TPU v7x, 32 devices: a whole 2x2x4 slice. The times are simulated.
32 devices in a mesh: frames: 8 (over y, x, core), rows: 4 (over z).
Axes of the slice: x: 2, y: 2, z: 4, core: 2. Of those that a mesh axis runs over, the one named last changes fastest.
Arguments:
- clip: bfloat16 [16, 32, 512, 256], P('frames', 'rows'), may hold values from -6 to 6
- w_query: bfloat16 [256, 256], replicated, may hold values from -32 to 32
- w_key: bfloat16 [256, 256], replicated, may hold values from -1 to 1
- w_value: bfloat16 [256, 256], replicated, may hold values from -0.375 to 0.375
- w_out: bfloat16 [256, 256], replicated, may hold values from -0.375 to 0.375
- w_conv: bfloat16 [3, 3, 256, 256], replicated, may hold values from -0.125 to 0.125
- conv_bias: float32 [256], replicated, may hold values from -3 to 3
Outputs:
- upsampled: bfloat16 [16, 64, 512, 128], P('frames', 'rows')
All inputs are finite; a program needn't handle non-finite values.
Results may differ from a plain program's by a relative error of at most 0.012.
Values may be sent and summed in bfloat16 or wider, within the bound.
A program may use at most 192 MiB of HBM per device.

v0:
```python
import functools
import math

import jax
import jax.numpy as jnp
from jax import lax
from jax.experimental import pallas as pl
from jax.experimental.pallas import tpu as pltpu
from jax.sharding import PartitionSpec as P

HEADS = 8
PAIRS = HEADS // 2
MESH = pl.DeviceIdType.MESH
NT = (((1,), (1,)), ((), ()))


def attend_block(x, wqv_t, wk, wo):
    frames, _, chans = x.shape
    n = frames * 8
    hd = chans // HEADS
    x = x.astype(jnp.float32)
    mean = jnp.mean(x, axis=-1, keepdims=True)
    centred = x - mean
    var = jnp.mean(centred * centred, axis=-1, keepdims=True)
    xn = centred * lax.rsqrt(var + 1e-6)
    xs = jnp.concatenate(
        [xn[:, :8].reshape(n, chans), xn[:, 8:].reshape(n, chans)], axis=0
    ).astype(jnp.bfloat16)
    qv = lax.dot_general(wqv_t, xs, NT, preferred_element_type=jnp.float32).astype(jnp.bfloat16)
    keys = jnp.dot(xs, wk, preferred_element_type=jnp.float32).astype(jnp.bfloat16)

    head_row = lax.broadcasted_iota(jnp.int32, (chans, n), 0) // hd
    even = (head_row % 2 == 0).astype(jnp.float32).astype(jnp.bfloat16)
    odd = (head_row % 2 == 1).astype(jnp.float32).astype(jnp.bfloat16)
    pair_col = lax.broadcasted_iota(jnp.int32, (n, chans), 1) // (2 * hd)
    own = lax.broadcasted_iota(jnp.int32, (8, 2 * n), 0) == (
        lax.broadcasted_iota(jnp.int32, (8, 2 * n), 1) % 8
    )
    scale = math.log2(math.e) / math.sqrt(hd)

    attended = []
    for g in range(2):
        cols = slice(g * n, (g + 1) * n)
        q_t, v_t, k = qv[:chans, cols], qv[chans:, cols], keys[cols]
        rhs = jnp.concatenate([q_t * even, q_t * odd], axis=1)
        lhs = jnp.concatenate(
            [
                k * (pair_col == j).astype(jnp.float32).astype(jnp.bfloat16)
                for j in range(PAIRS)
            ],
            axis=0,
        )
        s = jnp.dot(lhs, rhs, preferred_element_type=jnp.float32)
        pieces = []
        for j in range(PAIRS):
            sj = s[j * n:(j + 1) * n].reshape(frames, 8, 2 * n)
            top = jnp.max(sj, axis=0, keepdims=True)
            e = jnp.exp2((sj - top) * scale)
            total = jnp.sum(e, axis=0)
            inv = jnp.where(own, 1.0 / total, 0.0)
            p = (e * inv[None]).reshape(n, 2 * n).astype(jnp.bfloat16)
            o = jnp.dot(v_t[2 * hd * j:2 * hd * (j + 1)], p, preferred_element_type=jnp.float32)
            pieces += [o[:hd, :n], o[hd:, n:]]
        attended.append(jnp.concatenate(pieces, axis=0).T)
    attended = jnp.concatenate(attended, axis=0).astype(jnp.bfloat16)
    out = jnp.dot(attended, wo, preferred_element_type=jnp.float32)
    return jnp.concatenate(
        [out[:n].reshape(frames, 8, chans), out[n:].reshape(frames, 8, chans)], axis=1
    ).astype(jnp.bfloat16)


def kernel(
    sizes, clip, wq, wk, wv, wo, wc, bias, out,
    clipv, xr, pr, back, act, stage, wqv_t,
    clip_sem, f_send, f_recv, b_send, b_recv, h_send, h_recv, o_sem,
):
    n_dev, n_strip, fl, rows, width, chans = sizes
    pw = width // n_dev
    me = lax.axis_index("frames")
    strip = lax.axis_index("rows")
    mine = pl.multiple_of(me * pw, pw)

    def peer(k):
        return lax.rem(me + k, n_dev)

    def forward(r, k):
        to = peer(k)
        return pltpu.make_async_remote_copy(
            src_ref=clip.at[:, r, pl.ds(pl.multiple_of(to * pw, pw), pw), :],
            dst_ref=xr.at[r, pl.ds(me * fl, fl)],
            send_sem=f_send.at[r, k],
            recv_sem=f_recv.at[r, k],
            device_id={"frames": to},
            device_id_type=MESH,
        )

    def forward_own(r):
        return pltpu.make_async_copy(
            clip.at[:, r, pl.ds(mine, pw), :], xr.at[r, pl.ds(me * fl, fl)], f_recv.at[r, 0]
        )

    def backward(r, k):
        to = peer(k)
        return pltpu.make_async_remote_copy(
            src_ref=pr.at[r, pl.ds(to * fl, fl)],
            dst_ref=back.at[r, :, pl.ds(mine, pw), :],
            send_sem=b_send.at[r, k],
            recv_sem=b_recv.at[r, k],
            device_id={"frames": to},
            device_id_type=MESH,
        )

    def backward_own(r):
        return pltpu.make_async_copy(
            pr.at[r, pl.ds(me * fl, fl)], back.at[r, :, pl.ds(mine, pw), :], b_recv.at[r, 0]
        )

    def halo(down):
        src, dst = (rows, 0) if down else (1, rows + 1)
        return pltpu.make_async_remote_copy(
            src_ref=act.at[src, :, :, pl.ds(chans, chans)],
            dst_ref=act.at[dst, :, :, pl.ds(chans, chans)],
            send_sem=h_send.at[int(down)],
            recv_sem=h_recv.at[int(down)],
            device_id={"rows": strip + 1 if down else strip - 1},
            device_id_type=MESH,
        )

    def order(i):
        return jnp.where(i == 0, 0, jnp.where(i == 1, rows - 1, i - 1))

    has_prev, has_next = strip > 0, strip < n_strip - 1

    barrier = pltpu.get_barrier_semaphore()

    @pl.loop(1, n_dev)
    def _(k):
        pl.semaphore_signal(barrier, inc=1, device_id={"frames": peer(k)}, device_id_type=MESH)

    @pl.when(has_prev)
    def _():
        pl.semaphore_signal(barrier, inc=1, device_id={"rows": strip - 1}, device_id_type=MESH)

    @pl.when(has_next)
    def _():
        pl.semaphore_signal(barrier, inc=1, device_id={"rows": strip + 1}, device_id_type=MESH)

    @pl.loop(0, rows)
    def _(i):
        forward_own(order(i)).start()

    pl.semaphore_wait(
        barrier, n_dev - 1 + has_prev.astype(jnp.int32) + has_next.astype(jnp.int32)
    )

    @pl.loop(0, rows)
    def _(i):
        @pl.loop(1, n_dev)
        def _(k):
            forward(order(i), k).start()

    whole = pltpu.make_async_copy(clip, clipv, clip_sem)
    whole.start()
    wqv_t[:chans] = wq[...].astype(jnp.float32).T.astype(jnp.bfloat16)
    wqv_t[chans:] = wv[...].astype(jnp.float32).T.astype(jnp.bfloat16)

    @pl.loop(0, rows)
    def _(i):
        r = order(i)
        forward_own(r).wait()

        @pl.loop(1, n_dev)
        def _(k):
            forward(r, k).wait_recv()

        @pl.loop(0, pw // 16)
        def _(b):
            at = pl.ds(pl.multiple_of(b * 16, 16), 16)
            pr[r, :, at, :] = attend_block(xr[r, :, at, :], wqv_t[...], wk[...], wo[...])

        @pl.loop(1, n_dev)
        def _(k):
            backward(r, k).start()

        backward_own(r).start()

    whole.wait()

    def spread(a, row, f):
        pixel = lax.broadcasted_iota(jnp.int32, a.shape, 0)
        before = jnp.where(pixel == 0, 0.0, pltpu.roll(a, 1, 0))
        after = jnp.where(pixel == width - 1, 0.0, pltpu.roll(a, width - 1, 0))
        act[row, f, :, pl.ds(0, chans)] = before.astype(jnp.bfloat16)
        act[row, f, :, pl.ds(2 * chans, chans)] = after.astype(jnp.bfloat16)

    def activate(r):
        backward_own(r).wait()

        @pl.loop(1, n_dev)
        def _(k):
            backward(r, k).wait_recv()

        @pl.loop(0, fl)
        def _(f):
            h = clipv[f, r].astype(jnp.float32) + back[r, f].astype(jnp.float32)
            half = 0.5 * h
            a = half + half * jnp.tanh(half)
            act[r + 1, f, :, pl.ds(chans, chans)] = a.astype(jnp.bfloat16)
            spread(a, r + 1, f)

    def out_copy(r):
        return pltpu.make_async_copy(
            stage.at[:, pl.ds(2 * r, 2)], out.at[:, pl.ds(2 * r, 2)], o_sem.at[r]
        )

    def convolve(r):
        tile = min(width, 256)

        @pl.loop(0, fl)
        def _(f):
            @pl.loop(0, width // tile)
            def _(t):
                at = pl.ds(pl.multiple_of(t * tile, tile), tile)
                total = clipv[f, r, at, :].astype(jnp.float32) + back[r, f, at, :].astype(jnp.float32)
                total = total + bias[...]
                for d in range(3):
                    total = total + jnp.dot(
                        act[r + d, f, at, :], wc[d], preferred_element_type=jnp.float32
                    )
                mixed = total.astype(jnp.bfloat16)
                stage[f, 2 * r, at, :] = mixed[:, :chans // 2]
                stage[f, 2 * r + 1, at, :] = mixed[:, chans // 2:]

        out_copy(r).start()

    @pl.loop(0, 2)
    def _(i):
        activate(i * (rows - 1))

    @pl.when(has_prev)
    def _():
        halo(False).start()

    @pl.when(has_next)
    def _():
        halo(True).start()

    activate(1)

    @pl.loop(1, rows - 2)
    def _(r):
        activate(r + 1)
        convolve(r)

    def spread_halo(row):
        @pl.loop(0, fl)
        def _(f):
            spread(act[row, f, :, pl.ds(chans, chans)].astype(jnp.float32), row, f)

    def clear(row):
        act[row] = jnp.zeros(act.shape[1:], act.dtype)

    @pl.when(has_prev)
    def _():
        halo(True).wait_recv()
        spread_halo(0)

    @pl.when(jnp.logical_not(has_prev))
    def _():
        clear(0)

    @pl.when(has_next)
    def _():
        halo(False).wait_recv()
        spread_halo(rows + 1)

    @pl.when(jnp.logical_not(has_next))
    def _():
        clear(rows + 1)

    @pl.loop(0, 3)
    def _(i):
        convolve(lax.rem(i + rows - 2, rows))

    @pl.loop(0, rows)
    def _(r):
        @pl.loop(1, n_dev)
        def _(k):
            forward(r, k).wait_send()
            backward(r, k).wait_send()

        out_copy(r).wait()

    @pl.when(has_prev)
    def _():
        halo(False).wait_send()

    @pl.when(has_next)
    def _():
        halo(True).wait_send()


def local(n_dev, n_strip, clip, w_query, w_key, w_value, w_out, w_conv, conv_bias):
    fl, rows, width, chans = clip.shape
    frames = fl * n_dev
    pw = width // n_dev
    sizes = (n_dev, n_strip, fl, rows, width, chans)
    bf16 = jnp.bfloat16
    vmem = pl.BlockSpec(memory_space=pltpu.VMEM)
    hbm = pl.BlockSpec(memory_space=pl.ANY)
    positions = fl * rows * width
    return pl.pallas_call(
        functools.partial(kernel, sizes),
        out_shape=jax.ShapeDtypeStruct((fl, 2 * rows, width, chans // 2), bf16),
        in_specs=[hbm] + [vmem] * 6,
        out_specs=hbm,
        scratch_shapes=[
            pltpu.VMEM((fl, rows, width, chans), bf16),
            pltpu.VMEM((rows, frames, pw, chans), bf16),
            pltpu.VMEM((rows, frames, pw, chans), bf16),
            pltpu.VMEM((rows, fl, width, chans), bf16),
            pltpu.VMEM((rows + 2, fl, width, 3 * chans), bf16),
            pltpu.VMEM((fl, 2 * rows, width, chans // 2), bf16),
            pltpu.VMEM((2 * chans, chans), bf16),
            pltpu.SemaphoreType.DMA,
            pltpu.SemaphoreType.DMA((rows, n_dev)),
            pltpu.SemaphoreType.DMA((rows, n_dev)),
            pltpu.SemaphoreType.DMA((rows, n_dev)),
            pltpu.SemaphoreType.DMA((rows, n_dev)),
            pltpu.SemaphoreType.DMA((2,)),
            pltpu.SemaphoreType.DMA((2,)),
            pltpu.SemaphoreType.DMA((rows,)),
        ],
        compiler_params=pltpu.CompilerParams(
            collective_id=0, has_side_effects=True, vmem_limit_bytes=58 * 1024 * 1024
        ),
        cost_estimate=pl.CostEstimate(
            flops=positions * chans * chans * 2 * 13,
            bytes_accessed=positions * chans * 2 * 4,
            transcendentals=positions * chans * 8,
        ),
    )(
        clip, w_query, w_key, w_value, w_out,
        w_conv.reshape(3, 3 * chans, chans), conv_bias.reshape(1, chans),
    )


def solution(mesh):
    placed = (P("frames", "rows", None, None), P(), P(), P(), P(), P(), P())
    return jax.shard_map(
        functools.partial(local, mesh.shape["frames"], mesh.shape["rows"]),
        mesh=mesh,
        in_specs=placed,
        out_specs=P("frames", "rows", None, None),
        check_vma=False,
    )
```

profile of v0, /device:TPU:1, one launch (start us, length us, event | category | flops | bytes accessed | tf_op | source)
XLA Modules:
  0.0 114.1 jit_solution(18199615759335800580)
XLA Ops:
  0.0 109.4 %shard_map.73 = bf16[2,16,512,128]{3,2,1,0:T(8,128)(2,1)} custom-call(bf16[2,8,512,256]{3,2,1,0:T(8,128)(2,1)} %clip.1, bf16[256,256]{1,0:T(8,128)(2,1)} %wq.1, bf16[256,256]{1,0:T(8,128)(2,1)} %wk.1, bf16[256,256]{1,0:T(8,128)(2,1)} %wv.1, bf16[256,256]{1,0:T(8,128)(2,1)} %wo.1, bf16[3,768,256]{2,1,0:T(8,128)(2,1)} %bitcast.2, f32[1,256]{1,0:T(1,128)} %bitcast.3), custom_call_target="tpu_custom_call" | custom-call | flops 13958643712 | bytes 16777216 | tf_op jit(solution)/shard_map/pallas_call | solution.py:312
  109.4 4.7 %copy.9 = bf16[2,16,512,128]{3,2,1,0:T(8,128)(2,1)} copy(bf16[2,16,512,128]{3,2,1,0:T(8,128)(2,1)} %shard_map.73) | data formatting | bytes 8388608
where the time goes:
time: 114 us
  Pallas kernels  109 us (96%)
  local copies, waits for them, and re-layouts  4.65 us (4%)
    pallas_call x1, Pallas kernels, local(): pl.pallas_call(functools.partial(kernel, sizes), out_shape=jax.ShapeDtype...  109 us
    unnamed x1, local copies, waits for them, and re-layouts  4.65 us

commit v1 on v0

--- a/solution.py
+++ b/solution.py
@@ -10,6 +10,7 @@
 
 HEADS = 8
 PAIRS = HEADS // 2
+LAG = 4
 MESH = pl.DeviceIdType.MESH
 NT = (((1,), (1,)), ((), ()))
 
@@ -69,10 +70,18 @@
     ).astype(jnp.bfloat16)
 
 
+def offsets(n_dev):
+    chips = list(range(1, n_dev // 2))
+    swapped = list(chips)
+    for i in range(0, len(chips) - 1, 2):
+        swapped[i], swapped[i + 1] = chips[i + 1], chips[i]
+    return [[2 * chip + half for half in range(2) for chip in c] + [1] for c in (chips, swapped)]
+
+
 def kernel(
     sizes, clip, wq, wk, wv, wo, wc, bias, out,
-    clipv, xr, pr, back, act, stage, wqv_t,
-    clip_sem, f_send, f_recv, b_send, b_recv, h_send, h_recv, o_sem,
+    clipv, xr, pr, back, act, wqv_t,
+    clip_sem, f_send, f_recv, b_send, b_recv, h_send, h_recv,
 ):
     n_dev, n_strip, fl, rows, width, chans = sizes
     pw = width // n_dev
@@ -81,7 +90,16 @@
     mine = pl.multiple_of(me * pw, pw)
 
     def peer(k):
-        return lax.rem(me + k, n_dev)
+        out = 0
+        for bit in range(n_dev.bit_length() - 1):
+            one = 1 << bit
+            out = out + lax.rem(lax.div(me, one) + lax.div(k, one), 2) * one
+        return out
+
+    def start_to_all(copy, r):
+        core = lax.rem(me, 2)
+        for a, b in zip(*offsets(n_dev)):
+            copy(r, jnp.where(core == 0, a, b)).start()
 
     def forward(r, k):
         to = peer(k)
@@ -155,18 +173,14 @@
 
     @pl.loop(0, rows)
     def _(i):
-        @pl.loop(1, n_dev)
-        def _(k):
-            forward(order(i), k).start()
+        start_to_all(forward, order(i))
 
     whole = pltpu.make_async_copy(clip, clipv, clip_sem)
     whole.start()
     wqv_t[:chans] = wq[...].astype(jnp.float32).T.astype(jnp.bfloat16)
     wqv_t[chans:] = wv[...].astype(jnp.float32).T.astype(jnp.bfloat16)
 
-    @pl.loop(0, rows)
-    def _(i):
-        r = order(i)
+    def attend(r):
         forward_own(r).wait()
 
         @pl.loop(1, n_dev)
@@ -178,13 +192,8 @@
             at = pl.ds(pl.multiple_of(b * 16, 16), 16)
             pr[r, :, at, :] = attend_block(xr[r, :, at, :], wqv_t[...], wk[...], wo[...])
 
-        @pl.loop(1, n_dev)
-        def _(k):
-            backward(r, k).start()
-
+        start_to_all(backward, r)
         backward_own(r).start()
-
-    whole.wait()
 
     def spread(a, row, f):
         pixel = lax.broadcasted_iota(jnp.int32, a.shape, 0)
@@ -207,11 +216,6 @@
             a = half + half * jnp.tanh(half)
             act[r + 1, f, :, pl.ds(chans, chans)] = a.astype(jnp.bfloat16)
             spread(a, r + 1, f)
-
-    def out_copy(r):
-        return pltpu.make_async_copy(
-            stage.at[:, pl.ds(2 * r, 2)], out.at[:, pl.ds(2 * r, 2)], o_sem.at[r]
-        )
 
     def convolve(r):
         tile = min(width, 256)
@@ -228,29 +232,8 @@
                         act[r + d, f, at, :], wc[d], preferred_element_type=jnp.float32
                     )
                 mixed = total.astype(jnp.bfloat16)
-                stage[f, 2 * r, at, :] = mixed[:, :chans // 2]
-                stage[f, 2 * r + 1, at, :] = mixed[:, chans // 2:]
-
-        out_copy(r).start()
-
-    @pl.loop(0, 2)
-    def _(i):
-        activate(i * (rows - 1))
-
-    @pl.when(has_prev)
-    def _():
-        halo(False).start()
-
-    @pl.when(has_next)
-    def _():
-        halo(True).start()
-
-    activate(1)
-
-    @pl.loop(1, rows - 2)
-    def _(r):
-        activate(r + 1)
-        convolve(r)
+                out[f, 2 * r, at, :] = mixed[:, :chans // 2]
+                out[f, 2 * r + 1, at, :] = mixed[:, chans // 2:]
 
     def spread_halo(row):
         @pl.loop(0, fl)
@@ -260,27 +243,65 @@
     def clear(row):
         act[row] = jnp.zeros(act.shape[1:], act.dtype)
 
-    @pl.when(has_prev)
-    def _():
-        halo(True).wait_recv()
-        spread_halo(0)
-
-    @pl.when(jnp.logical_not(has_prev))
-    def _():
-        clear(0)
-
-    @pl.when(has_next)
-    def _():
-        halo(False).wait_recv()
-        spread_halo(rows + 1)
-
-    @pl.when(jnp.logical_not(has_next))
-    def _():
-        clear(rows + 1)
-
-    @pl.loop(0, 3)
+    def finish_halo():
+        @pl.when(has_prev)
+        def _():
+            halo(True).wait_recv()
+            spread_halo(0)
+
+        @pl.when(jnp.logical_not(has_prev))
+        def _():
+            clear(0)
+
+        @pl.when(has_next)
+        def _():
+            halo(False).wait_recv()
+            spread_halo(rows + 1)
+
+        @pl.when(jnp.logical_not(has_next))
+        def _():
+            clear(rows + 1)
+
+    def send_halo():
+        @pl.when(has_prev)
+        def _():
+            halo(False).start()
+
+        @pl.when(has_next)
+        def _():
+            halo(True).start()
+
+    whole.wait()
+
+    @pl.loop(0, rows + LAG)
     def _(i):
-        convolve(lax.rem(i + rows - 2, rows))
+        @pl.when(i < rows)
+        def _():
+            attend(order(i))
+
+        j = i - LAG
+
+        @pl.when(j >= 0)
+        def _():
+            activate(order(j))
+
+        @pl.when(j == 1)
+        def _():
+            send_halo()
+
+        @pl.when(j == 5)
+        def _():
+            finish_halo()
+
+        @pl.when(j >= 3)
+        def _():
+            @pl.loop(0, jnp.where(j == 5, 2, 1))
+            def _(second):
+                convolve(jnp.where(second == 0, j - 2, 0))
+
+    @pl.loop(rows - 2, rows)
+    def _(r):
+        convolve(r)
 
     @pl.loop(0, rows)
     def _(r):
@@ -288,8 +309,6 @@
         def _(k):
             forward(r, k).wait_send()
             backward(r, k).wait_send()
-
-        out_copy(r).wait()
 
     @pl.when(has_prev)
     def _():
@@ -311,16 +330,15 @@
     positions = fl * rows * width
     return pl.pallas_call(
         functools.partial(kernel, sizes),
-        out_shape=jax.ShapeDtypeStruct((fl, 2 * rows, width, chans // 2), bf16),
+        out_shape=pltpu.VMEM((fl, 2 * rows, width, chans // 2), bf16),
         in_specs=[hbm] + [vmem] * 6,
-        out_specs=hbm,
+        out_specs=vmem,
         scratch_shapes=[
             pltpu.VMEM((fl, rows, width, chans), bf16),
             pltpu.VMEM((rows, frames, pw, chans), bf16),
             pltpu.VMEM((rows, frames, pw, chans), bf16),
             pltpu.VMEM((rows, fl, width, chans), bf16),
             pltpu.VMEM((rows + 2, fl, width, 3 * chans), bf16),
-            pltpu.VMEM((fl, 2 * rows, width, chans // 2), bf16),
             pltpu.VMEM((2 * chans, chans), bf16),
             pltpu.SemaphoreType.DMA,
             pltpu.SemaphoreType.DMA((rows, n_dev)),
@@ -329,10 +347,9 @@
             pltpu.SemaphoreType.DMA((rows, n_dev)),
             pltpu.SemaphoreType.DMA((2,)),
             pltpu.SemaphoreType.DMA((2,)),
-            pltpu.SemaphoreType.DMA((rows,)),
         ],
         compiler_params=pltpu.CompilerParams(
-            collective_id=0, has_side_effects=True, vmem_limit_bytes=58 * 1024 * 1024
+            collective_id=0, has_side_effects=True, vmem_limit_bytes=48 * 1024 * 1024
         ),
         cost_estimate=pl.CostEstimate(
             flops=positions * chans * chans * 2 * 13,

time: 114 us -> 112 us (0.982)
  Pallas kernels: 109 us -> 105 us
  local copies, waits for them, and re-layouts: 4.65 us -> 7.58 us
    pallas_call x1, Pallas kernels: 109 us -> 105 us  [local(): pl.pallas_call(functools.partial(kernel, sizes), out_shape=pltpu.VMEM((fl...]
    unnamed x1 -> x13, local copies, waits for them, and re-layouts: 4.65 us -> 7.58 us
where the time goes in v1:
time: 112 us
  Pallas kernels  105 us (94%)
  local copies, waits for them, and re-layouts  7.58 us (7%)
    pallas_call x1, Pallas kernels, local(): pl.pallas_call(functools.partial(kernel, sizes), out_shape=pltpu.VMEM((fl...  105 us
    unnamed x13, local copies, waits for them, and re-layouts  7.58 us

profile of v1, /device:TPU:1, one launch (start us, length us, event | category | flops | bytes accessed | tf_op | source)
XLA Modules:
  0.0 112.1 jit_solution(6370489688793035507)
XLA Ops:
  0.0 0.0 copy-start
  0.0 1.3 %copy-done = bf16[3,3,256,256]{3,2,1,0:T(8,128)(2,1)S(1)} copy-done((bf16[3,3,256,256]{3,2,1,0:T(8,128)(2,1)S(1)}, bf16[3,3,256,256]{3,2,1,0:T(8,128)(2,1)}, u32[]{:S(2)}) %copy-start) | copy-done | bytes 1179672
  1.3 0.0 copy-start.1
  1.3 0.9 copy-done.1
  2.2 0.0 copy-start.2
  2.2 0.9 copy-done.2
  3.1 0.0 copy-start.3
  3.1 0.9 copy-done.3
  4.0 0.0 copy-start.4
  4.0 0.9 copy-done.4
  4.9 0.0 copy-start.5
  4.9 0.7 copy-done.5
  5.6 104.5 %shard_map.73 = bf16[2,16,512,128]{3,2,1,0:T(8,128)(2,1)S(1)} custom-call(bf16[2,8,512,256]{3,2,1,0:T(8,128)(2,1)} %clip.1, bf16[256,256]{1,0:T(8,128)(2,1)S(1)} %copy-done.1, bf16[256,256]{1,0:T(8,128)(2,1)S(1)} %copy-done.2, bf16[256,256]{1,0:T(8,128)(2,1)S(1)} %copy-done.3, bf16[256,256]{1,0:T(8,128)(2,1)S(1)} %copy-done.4, ...), custom_call_target="tpu_custom_call" | custom-call | flops 13958643712 | bytes 16777216 | tf_op jit(solution)/shard_map/pallas_call | solution.py:331
  110.1 2.0 %copy.9 = bf16[2,16,512,128]{3,2,1,0:T(8,128)(2,1)} copy(bf16[2,16,512,128]{3,2,1,0:T(8,128)(2,1)S(1)} %shard_map.73) | data formatting | bytes 8388608
Async XLA Ops:
  0.0 1.3 %copy-start = (bf16[3,3,256,256]{3,2,1,0:T(8,128)(2,1)S(1)}, bf16[3,3,256,256]{3,2,1,0:T(8,128)(2,1)}, u32[]{:S(2)}) copy-start(bf16[3,3,256,256]{3,2,1,0:T(8,128)(2,1)} %param.12) | copy-start | bytes 3538948
  1.3 0.9 copy-start.1
  2.2 0.9 copy-start.2
  3.1 0.9 copy-start.3
  4.0 0.9 copy-start.4
  4.9 0.7 copy-start.5

commit v2 on v1

--- a/solution.py
+++ b/solution.py
@@ -16,45 +16,55 @@
 
 
 def attend_block(x, wqv_t, wk, wo):
-    frames, _, chans = x.shape
+    frames, pixels, chans = x.shape
     n = frames * 8
+    groups = pixels // 8
     hd = chans // HEADS
+    half = chans // 2
     x = x.astype(jnp.float32)
     mean = jnp.mean(x, axis=-1, keepdims=True)
     centred = x - mean
     var = jnp.mean(centred * centred, axis=-1, keepdims=True)
     xn = centred * lax.rsqrt(var + 1e-6)
     xs = jnp.concatenate(
-        [xn[:, :8].reshape(n, chans), xn[:, 8:].reshape(n, chans)], axis=0
+        [xn[:, 8 * g:8 * g + 8].reshape(n, chans) for g in range(groups)], axis=0
     ).astype(jnp.bfloat16)
     qv = lax.dot_general(wqv_t, xs, NT, preferred_element_type=jnp.float32).astype(jnp.bfloat16)
     keys = jnp.dot(xs, wk, preferred_element_type=jnp.float32).astype(jnp.bfloat16)
 
-    head_row = lax.broadcasted_iota(jnp.int32, (chans, n), 0) // hd
-    even = (head_row % 2 == 0).astype(jnp.float32).astype(jnp.bfloat16)
-    odd = (head_row % 2 == 1).astype(jnp.float32).astype(jnp.bfloat16)
-    pair_col = lax.broadcasted_iota(jnp.int32, (n, chans), 1) // (2 * hd)
+    low = lax.broadcasted_iota(jnp.int32, (n, half), 1) < half // 2
+    first = jnp.where(low, 1.0, 0.0).astype(jnp.bfloat16)
+    second = jnp.where(low, 0.0, 1.0).astype(jnp.bfloat16)
+    none = jnp.zeros((hd, n), jnp.bfloat16)
     own = lax.broadcasted_iota(jnp.int32, (8, 2 * n), 0) == (
-        lax.broadcasted_iota(jnp.int32, (8, 2 * n), 1) % 8
+        lax.broadcasted_iota(jnp.int32, (8, 2 * n), 1) & 7
     )
     scale = math.log2(math.e) / math.sqrt(hd)
 
-    attended = []
-    for g in range(2):
-        cols = slice(g * n, (g + 1) * n)
-        q_t, v_t, k = qv[:chans, cols], qv[chans:, cols], keys[cols]
-        rhs = jnp.concatenate([q_t * even, q_t * odd], axis=1)
-        lhs = jnp.concatenate(
-            [
-                k * (pair_col == j).astype(jnp.float32).astype(jnp.bfloat16)
-                for j in range(PAIRS)
-            ],
-            axis=0,
-        )
-        s = jnp.dot(lhs, rhs, preferred_element_type=jnp.float32)
+    def scores(g):
+        q_t, k = qv[:chans, g * n:(g + 1) * n], keys[g * n:(g + 1) * n]
+        out = []
+        for side in range(2):
+            heads = [
+                q_t[side * half + hd * h:side * half + hd * (h + 1)] for h in range(HEADS // 2)
+            ]
+            rhs = jnp.concatenate(
+                [
+                    jnp.concatenate([q if h % 2 == parity else none for h, q in enumerate(heads)], axis=0)
+                    for parity in range(2)
+                ],
+                axis=1,
+            )
+            k_side = k[:, side * half:(side + 1) * half]
+            lhs = jnp.concatenate([k_side * first, k_side * second], axis=0)
+            out.append(jnp.dot(lhs, rhs, preferred_element_type=jnp.float32))
+        return out
+
+    def weigh(g, s):
+        v_t = qv[chans:, g * n:(g + 1) * n]
         pieces = []
         for j in range(PAIRS):
-            sj = s[j * n:(j + 1) * n].reshape(frames, 8, 2 * n)
+            sj = s[j // 2][(j % 2) * n:(j % 2 + 1) * n].reshape(frames, 8, 2 * n)
             top = jnp.max(sj, axis=0, keepdims=True)
             e = jnp.exp2((sj - top) * scale)
             total = jnp.sum(e, axis=0)
@@ -62,11 +72,19 @@
             p = (e * inv[None]).reshape(n, 2 * n).astype(jnp.bfloat16)
             o = jnp.dot(v_t[2 * hd * j:2 * hd * (j + 1)], p, preferred_element_type=jnp.float32)
             pieces += [o[:hd, :n], o[hd:, n:]]
-        attended.append(jnp.concatenate(pieces, axis=0).T)
+        return jnp.concatenate(pieces, axis=0).T
+
+    attended = []
+    ahead = scores(0)
+    for g in range(groups):
+        now = ahead
+        if g + 1 < groups:
+            ahead = scores(g + 1)
+        attended.append(weigh(g, now))
     attended = jnp.concatenate(attended, axis=0).astype(jnp.bfloat16)
     out = jnp.dot(attended, wo, preferred_element_type=jnp.float32)
     return jnp.concatenate(
-        [out[:n].reshape(frames, 8, chans), out[n:].reshape(frames, 8, chans)], axis=1
+        [out[g * n:(g + 1) * n].reshape(frames, 8, chans) for g in range(groups)], axis=1
     ).astype(jnp.bfloat16)
 
 
@@ -79,9 +97,9 @@
 
 
 def kernel(
-    sizes, clip, wq, wk, wv, wo, wc, bias, out,
-    clipv, xr, pr, back, act, wqv_t,
-    clip_sem, f_send, f_recv, b_send, b_recv, h_send, h_recv,
+    sizes, clip, wq_in, wk_in, wv_in, wo_in, wc_in, bias_in, out,
+    clipv, xr, pr, back, act, part, wqv_t, wq, wk, wv, wo, wc, bias,
+    clip_sem, w_sem, f_send, f_recv, b_send, b_recv, h_send, h_recv,
 ):
     n_dev, n_strip, fl, rows, width, chans = sizes
     pw = width // n_dev
@@ -149,6 +167,13 @@
 
     has_prev, has_next = strip > 0, strip < n_strip - 1
 
+    weights = [
+        pltpu.make_async_copy(src, dst, w_sem.at[i])
+        for i, (src, dst) in enumerate(
+            [(wq_in, wq), (wv_in, wv), (wk_in, wk), (wo_in, wo), (wc_in, wc), (bias_in, bias)]
+        )
+    ]
+
     barrier = pltpu.get_barrier_semaphore()
 
     @pl.loop(1, n_dev)
@@ -163,6 +188,9 @@
     def _():
         pl.semaphore_signal(barrier, inc=1, device_id={"rows": strip + 1}, device_id_type=MESH)
 
+    for copy in weights:
+        copy.start()
+
     @pl.loop(0, rows)
     def _(i):
         forward_own(order(i)).start()
@@ -177,6 +205,8 @@
 
     whole = pltpu.make_async_copy(clip, clipv, clip_sem)
     whole.start()
+    for copy in weights:
+        copy.wait()
     wqv_t[:chans] = wq[...].astype(jnp.float32).T.astype(jnp.bfloat16)
     wqv_t[chans:] = wv[...].astype(jnp.float32).T.astype(jnp.bfloat16)
 
@@ -187,9 +217,11 @@
         def _(k):
             forward(r, k).wait_recv()
 
-        @pl.loop(0, pw // 16)
+        block = min(pw, 32)
+
+        @pl.loop(0, pw // block)
         def _(b):
-            at = pl.ds(pl.multiple_of(b * 16, 16), 16)
+            at = pl.ds(pl.multiple_of(b * block, block), block)
             pr[r, :, at, :] = attend_block(xr[r, :, at, :], wqv_t[...], wk[...], wo[...])
 
         start_to_all(backward, r)
@@ -217,23 +249,39 @@
             act[r + 1, f, :, pl.ds(chans, chans)] = a.astype(jnp.bfloat16)
             spread(a, r + 1, f)
 
-    def convolve(r):
+    def tiles(body):
         tile = min(width, 256)
 
         @pl.loop(0, fl)
         def _(f):
             @pl.loop(0, width // tile)
             def _(t):
-                at = pl.ds(pl.multiple_of(t * tile, tile), tile)
-                total = clipv[f, r, at, :].astype(jnp.float32) + back[r, f, at, :].astype(jnp.float32)
-                total = total + bias[...]
-                for d in range(3):
-                    total = total + jnp.dot(
-                        act[r + d, f, at, :], wc[d], preferred_element_type=jnp.float32
-                    )
-                mixed = total.astype(jnp.bfloat16)
-                out[f, 2 * r, at, :] = mixed[:, :chans // 2]
-                out[f, 2 * r + 1, at, :] = mixed[:, chans // 2:]
+                body(f, pl.ds(pl.multiple_of(t * tile, tile), tile))
+
+    def taps(r, d, f, at):
+        return jnp.dot(act[r + d, f, at, :], wc[d], preferred_element_type=jnp.float32)
+
+    def finish(r, f, at, convolved):
+        hidden = clipv[f, r, at, :].astype(jnp.float32) + back[r, f, at, :].astype(jnp.float32)
+        mixed = (hidden + convolved + bias[...]).astype(jnp.bfloat16)
+        out[f, 2 * r, at, :] = mixed[:, :chans // 2]
+        out[f, 2 * r + 1, at, :] = mixed[:, chans // 2:]
+
+    def convolve(r):
+        tiles(lambda f, at: finish(r, f, at, sum(taps(r, d, f, at) for d in range(3))))
+
+    def begin_last(t):
+        r = rows - 3 + t
+        one, two = t // 2, 1 + (t + 1) // 2
+
+        def body(f, at):
+            part[t, f, at, :] = taps(r, one, f, at) + taps(r, two, f, at)
+
+        tiles(body)
+
+    def finish_last(t):
+        r = rows - 3 + t
+        tiles(lambda f, at: finish(r, f, at, part[t, f, at, :] + taps(r, 2 - t, f, at)))
 
     def spread_halo(row):
         @pl.loop(0, fl)
@@ -281,6 +329,12 @@
 
         j = i - LAG
 
+        @pl.when(j == rows - 1)
+        def _():
+            @pl.loop(0, 3)
+            def _(t):
+                begin_last(t)
+
         @pl.when(j >= 0)
         def _():
             activate(order(j))
@@ -293,15 +347,15 @@
         def _():
             finish_halo()
 
-        @pl.when(j >= 3)
+        @pl.when(jnp.logical_and(j >= 3, j < rows - 1))
         def _():
             @pl.loop(0, jnp.where(j == 5, 2, 1))
             def _(second):
                 convolve(jnp.where(second == 0, j - 2, 0))
 
-    @pl.loop(rows - 2, rows)
-    def _(r):
-        convolve(r)
+    @pl.loop(0, 3)
+    def _(t):
+        finish_last(t)
 
     @pl.loop(0, rows)
     def _(r):
@@ -326,12 +380,12 @@
     sizes = (n_dev, n_strip, fl, rows, width, chans)
     bf16 = jnp.bfloat16
     vmem = pl.BlockSpec(memory_space=pltpu.VMEM)
-    hbm = pl.BlockSpec(memory_space=pl.ANY)
+    hbm = pl.BlockSpec(memory_space=pltpu.HBM)
     positions = fl * rows * width
     return pl.pallas_call(
         functools.partial(kernel, sizes),
         out_shape=pltpu.VMEM((fl, 2 * rows, width, chans // 2), bf16),
-        in_specs=[hbm] + [vmem] * 6,
+        in_specs=[hbm] * 7,
         out_specs=vmem,
         scratch_shapes=[
             pltpu.VMEM((fl, rows, width, chans), bf16),
@@ -339,8 +393,16 @@
             pltpu.VMEM((rows, frames, pw, chans), bf16),
             pltpu.VMEM((rows, fl, width, chans), bf16),
             pltpu.VMEM((rows + 2, fl, width, 3 * chans), bf16),
+            pltpu.VMEM((3, fl, width, chans), jnp.float32),
             pltpu.VMEM((2 * chans, chans), bf16),
+            pltpu.VMEM((chans, chans), bf16),
+            pltpu.VMEM((chans, chans), bf16),
+            pltpu.VMEM((chans, chans), bf16),
+            pltpu.VMEM((chans, chans), bf16),
+            pltpu.VMEM((3, 3 * chans, chans), bf16),
+            pltpu.VMEM((1, chans), jnp.float32),
             pltpu.SemaphoreType.DMA,
+            pltpu.SemaphoreType.DMA((6,)),
             pltpu.SemaphoreType.DMA((rows, n_dev)),
             pltpu.SemaphoreType.DMA((rows, n_dev)),
             pltpu.SemaphoreType.DMA((rows, n_dev)),
@@ -349,7 +411,7 @@
             pltpu.SemaphoreType.DMA((2,)),
         ],
         compiler_params=pltpu.CompilerParams(
-            collective_id=0, has_side_effects=True, vmem_limit_bytes=48 * 1024 * 1024
+            collective_id=0, has_side_effects=True, vmem_limit_bytes=59 * 1024 * 1024
         ),
         cost_estimate=pl.CostEstimate(
             flops=positions * chans * chans * 2 * 13,

time: 112 us -> 107 us (0.955)
  local copies, waits for them, and re-layouts: 7.58 us -> 2.02 us
    unnamed x13 -> x1, local copies, waits for them, and re-layouts: 7.58 us -> 2.02 us
where the time goes in v2:
time: 107 us
  Pallas kernels  105 us (98%)
  local copies, waits for them, and re-layouts  2.02 us (2%)
    pallas_call x1, Pallas kernels, local(): pl.pallas_call(functools.partial(kernel, sizes), out_shape=pltpu.VMEM((fl...  105 us

profile of v2, /device:TPU:1, one launch (start us, length us, event | category | flops | bytes accessed | tf_op | source)
XLA Modules:
  0.0 106.8 jit_solution(1987006407105762372)
XLA Ops:
  0.0 104.7 %shard_map.73 = bf16[2,16,512,128]{3,2,1,0:T(8,128)(2,1)S(1)} custom-call(bf16[2,8,512,256]{3,2,1,0:T(8,128)(2,1)} %clip.1, bf16[256,256]{1,0:T(8,128)(2,1)} %wq_in.1, bf16[256,256]{1,0:T(8,128)(2,1)} %wk_in.1, bf16[256,256]{1,0:T(8,128)(2,1)} %wv_in.1, bf16[256,256]{1,0:T(8,128)(2,1)} %wo_in.1, bf16[3,768,256]{2,1,0:T(8,128)(2,1)} %bitcast.2, f32[1,256]{1,0:T(1,128)} %bitcast.3), custom_call_target="tpu_custom_call" | custom-call | flops 13958643712 | bytes 16777216 | tf_op jit(solution)/shard_map/pallas_call | solution.py:385
  104.7 2.0 %copy.9 = bf16[2,16,512,128]{3,2,1,0:T(8,128)(2,1)} copy(bf16[2,16,512,128]{3,2,1,0:T(8,128)(2,1)S(1)} %shard_map.73) | data formatting | bytes 8388608

commit v3 on v2

--- a/solution.py
+++ b/solution.py
@@ -99,7 +99,7 @@
 def kernel(
     sizes, clip, wq_in, wk_in, wv_in, wo_in, wc_in, bias_in, out,
     clipv, xr, pr, back, act, part, wqv_t, wq, wk, wv, wo, wc, bias,
-    clip_sem, w_sem, f_send, f_recv, b_send, b_recv, h_send, h_recv,
+    clip_sem, w_sem, f_send, f_recv, b_send, b_recv, l_send, l_recv, h_send, h_recv,
 ):
     n_dev, n_strip, fl, rows, width, chans = sizes
     pw = width // n_dev
@@ -151,6 +151,24 @@
             pr.at[r, pl.ds(me * fl, fl)], back.at[r, :, pl.ds(mine, pw), :], b_recv.at[r, 0]
         )
 
+    last = rows - 2
+
+    def backward_frame(f, k):
+        to = peer(k)
+        return pltpu.make_async_remote_copy(
+            src_ref=pr.at[last, to * fl + f],
+            dst_ref=back.at[last, f, pl.ds(mine, pw), :],
+            send_sem=l_send.at[f, k],
+            recv_sem=l_recv.at[f, k],
+            device_id={"frames": to},
+            device_id_type=MESH,
+        )
+
+    def wait_sent(copy, r):
+        @pl.loop(1, n_dev)
+        def _(k):
+            copy(r, k).wait_send()
+
     def halo(down):
         src, dst = (rows, 0) if down else (1, rows + 1)
         return pltpu.make_async_remote_copy(
@@ -224,8 +242,17 @@
             at = pl.ds(pl.multiple_of(b * block, block), block)
             pr[r, :, at, :] = attend_block(xr[r, :, at, :], wqv_t[...], wk[...], wo[...])
 
-        start_to_all(backward, r)
         backward_own(r).start()
+
+        @pl.when(r != last)
+        def _():
+            start_to_all(backward, r)
+
+        @pl.when(r == last)
+        def _():
+            @pl.loop(0, fl)
+            def _(f):
+                start_to_all(backward_frame, f)
 
     def spread(a, row, f):
         pixel = lax.broadcasted_iota(jnp.int32, a.shape, 0)
@@ -234,6 +261,13 @@
         act[row, f, :, pl.ds(0, chans)] = before.astype(jnp.bfloat16)
         act[row, f, :, pl.ds(2 * chans, chans)] = after.astype(jnp.bfloat16)
 
+    def activate_frame(r, f):
+        h = clipv[f, r].astype(jnp.float32) + back[r, f].astype(jnp.float32)
+        half = 0.5 * h
+        a = half + half * jnp.tanh(half)
+        act[r + 1, f, :, pl.ds(chans, chans)] = a.astype(jnp.bfloat16)
+        spread(a, r + 1, f)
+
     def activate(r):
         backward_own(r).wait()
 
@@ -243,20 +277,19 @@
 
         @pl.loop(0, fl)
         def _(f):
-            h = clipv[f, r].astype(jnp.float32) + back[r, f].astype(jnp.float32)
-            half = 0.5 * h
-            a = half + half * jnp.tanh(half)
-            act[r + 1, f, :, pl.ds(chans, chans)] = a.astype(jnp.bfloat16)
-            spread(a, r + 1, f)
+            activate_frame(r, f)
+
+    def frame_tiles(f, body):
+        tile = min(width, 256)
+
+        @pl.loop(0, width // tile)
+        def _(t):
+            body(f, pl.ds(pl.multiple_of(t * tile, tile), tile))
 
     def tiles(body):
-        tile = min(width, 256)
-
         @pl.loop(0, fl)
         def _(f):
-            @pl.loop(0, width // tile)
-            def _(t):
-                body(f, pl.ds(pl.multiple_of(t * tile, tile), tile))
+            frame_tiles(f, body)
 
     def taps(r, d, f, at):
         return jnp.dot(act[r + d, f, at, :], wc[d], preferred_element_type=jnp.float32)
@@ -279,9 +312,9 @@
 
         tiles(body)
 
-    def finish_last(t):
+    def finish_last(t, f):
         r = rows - 3 + t
-        tiles(lambda f, at: finish(r, f, at, part[t, f, at, :] + taps(r, 2 - t, f, at)))
+        frame_tiles(f, lambda f, at: finish(r, f, at, part[t, f, at, :] + taps(r, 2 - t, f, at)))
 
     def spread_halo(row):
         @pl.loop(0, fl)
@@ -321,7 +354,7 @@
 
     whole.wait()
 
-    @pl.loop(0, rows + LAG)
+    @pl.loop(0, rows - 1 + LAG)
     def _(i):
         @pl.when(i < rows)
         def _():
@@ -329,25 +362,24 @@
 
         j = i - LAG
 
-        @pl.when(j == rows - 1)
-        def _():
-            @pl.loop(0, 3)
-            def _(t):
-                begin_last(t)
-
         @pl.when(j >= 0)
         def _():
             activate(order(j))
+            wait_sent(forward, order(j))
 
         @pl.when(j == 1)
         def _():
             send_halo()
 
+        @pl.when(j >= 2)
+        def _():
+            wait_sent(backward, order(j - 2))
+
         @pl.when(j == 5)
         def _():
             finish_halo()
 
-        @pl.when(jnp.logical_and(j >= 3, j < rows - 1))
+        @pl.when(j >= 3)
         def _():
             @pl.loop(0, jnp.where(j == 5, 2, 1))
             def _(second):
@@ -355,14 +387,13 @@
 
     @pl.loop(0, 3)
     def _(t):
-        finish_last(t)
-
-    @pl.loop(0, rows)
-    def _(r):
-        @pl.loop(1, n_dev)
-        def _(k):
-            forward(r, k).wait_send()
-            backward(r, k).wait_send()
+        begin_last(t)
+
+    @pl.loop(rows - 3, rows - 1)
+    def _(j):
+        wait_sent(backward, order(j))
+
+    wait_sent(forward, last)
 
     @pl.when(has_prev)
     def _():
@@ -371,6 +402,24 @@
     @pl.when(has_next)
     def _():
         halo(True).wait_send()
+
+    backward_own(last).wait()
+
+    @pl.loop(0, fl)
+    def _(f):
+        @pl.loop(1, n_dev)
+        def _(k):
+            backward_frame(f, k).wait_recv()
+
+        activate_frame(last, f)
+
+        @pl.loop(0, 3)
+        def _(t):
+            finish_last(t, f)
+
+    @pl.loop(0, fl)
+    def _(f):
+        wait_sent(backward_frame, f)
 
 
 def local(n_dev, n_strip, clip, w_query, w_key, w_value, w_out, w_conv, conv_bias):
@@ -407,6 +456,8 @@
             pltpu.SemaphoreType.DMA((rows, n_dev)),
             pltpu.SemaphoreType.DMA((rows, n_dev)),
             pltpu.SemaphoreType.DMA((rows, n_dev)),
+            pltpu.SemaphoreType.DMA((fl, n_dev)),
+            pltpu.SemaphoreType.DMA((fl, n_dev)),
             pltpu.SemaphoreType.DMA((2,)),
             pltpu.SemaphoreType.DMA((2,)),
         ],

time: 107 us -> 107 us (level)
  no operation moved by 1% of the time
where the time goes in v3:
time: 107 us
  Pallas kernels  105 us (98%)
  local copies, waits for them, and re-layouts  2.02 us (2%)
    pallas_call x1, Pallas kernels, local(): pl.pallas_call(functools.partial(kernel, sizes), out_shape=pltpu.VMEM((fl...  105 us

profile of v3, /device:TPU:1, one launch (start us, length us, event | category | flops | bytes accessed | tf_op | source)
XLA Modules:
  0.0 107.1 jit_solution(901564020174004300)
XLA Ops:
  0.0 105.1 %shard_map.73 = bf16[2,16,512,128]{3,2,1,0:T(8,128)(2,1)S(1)} custom-call(bf16[2,8,512,256]{3,2,1,0:T(8,128)(2,1)} %clip.1, bf16[256,256]{1,0:T(8,128)(2,1)} %wq_in.1, bf16[256,256]{1,0:T(8,128)(2,1)} %wk_in.1, bf16[256,256]{1,0:T(8,128)(2,1)} %wv_in.1, bf16[256,256]{1,0:T(8,128)(2,1)} %wo_in.1, bf16[3,768,256]{2,1,0:T(8,128)(2,1)} %bitcast.2, f32[1,256]{1,0:T(1,128)} %bitcast.3), custom_call_target="tpu_custom_call" | custom-call | flops 13958643712 | bytes 16777216 | tf_op jit(solution)/shard_map/pallas_call | solution.py:434
  105.1 2.0 %copy.9 = bf16[2,16,512,128]{3,2,1,0:T(8,128)(2,1)} copy(bf16[2,16,512,128]{3,2,1,0:T(8,128)(2,1)S(1)} %shard_map.73) | data formatting | bytes 8388608

commit v4 on v3

--- a/solution.py
+++ b/solution.py
@@ -9,7 +9,6 @@
 from jax.sharding import PartitionSpec as P
 
 HEADS = 8
-PAIRS = HEADS // 2
 LAG = 4
 MESH = pl.DeviceIdType.MESH
 NT = (((1,), (1,)), ((), ()))
@@ -60,27 +59,35 @@
             out.append(jnp.dot(lhs, rhs, preferred_element_type=jnp.float32))
         return out
 
-    def weigh(g, s):
-        v_t = qv[chans:, g * n:(g + 1) * n]
-        pieces = []
-        for j in range(PAIRS):
-            sj = s[j // 2][(j % 2) * n:(j % 2 + 1) * n].reshape(frames, 8, 2 * n)
-            top = jnp.max(sj, axis=0, keepdims=True)
-            e = jnp.exp2((sj - top) * scale)
-            total = jnp.sum(e, axis=0)
-            inv = jnp.where(own, 1.0 / total, 0.0)
-            p = (e * inv[None]).reshape(n, 2 * n).astype(jnp.bfloat16)
-            o = jnp.dot(v_t[2 * hd * j:2 * hd * (j + 1)], p, preferred_element_type=jnp.float32)
-            pieces += [o[:hd, :n], o[hd:, n:]]
-        return jnp.concatenate(pieces, axis=0).T
-
-    attended = []
-    ahead = scores(0)
-    for g in range(groups):
-        now = ahead
-        if g + 1 < groups:
-            ahead = scores(g + 1)
-        attended.append(weigh(g, now))
+    def probabilities(s):
+        s = s.reshape(2, frames, 8, 2 * n)
+        top = jnp.max(s, axis=1, keepdims=True)
+        e = jnp.exp2((s - top) * scale)
+        inv = jnp.where(own, 1.0 / jnp.sum(e, axis=1), 0.0)
+        return (e * inv[:, None]).reshape(2 * n, 2 * n).astype(jnp.bfloat16)
+
+    gap = jnp.zeros((2 * hd, n), jnp.bfloat16)
+
+    def weigh(g, side, p):
+        v_t = qv[chans + side * half:chans + (side + 1) * half, g * n:(g + 1) * n]
+        values = jnp.concatenate(
+            [
+                jnp.concatenate([v_t[:2 * hd], gap], axis=1),
+                jnp.concatenate([gap, v_t[2 * hd:]], axis=1),
+            ],
+            axis=0,
+        )
+        o = jnp.dot(values, p, preferred_element_type=jnp.float32)
+        return [
+            o[hd * h:hd * (h + 1), (h % 2) * n:(h % 2 + 1) * n] for h in range(HEADS // 2)
+        ]
+
+    everything = [scores(g) for g in range(groups)]
+    probs = [[probabilities(s) for s in sides] for sides in everything]
+    heads = [
+        weigh(g, 0, probs[g][0]) + weigh(g, 1, probs[g][1]) for g in range(groups)
+    ]
+    attended = [jnp.concatenate(h, axis=0).T for h in heads]
     attended = jnp.concatenate(attended, axis=0).astype(jnp.bfloat16)
     out = jnp.dot(attended, wo, preferred_element_type=jnp.float32)
     return jnp.concatenate(
@@ -280,7 +287,7 @@
             activate_frame(r, f)
 
     def frame_tiles(f, body):
-        tile = min(width, 256)
+        tile = min(width, 512)
 
         @pl.loop(0, width // tile)
         def _(t):

time: 107 us -> 105 us (0.981)
  Pallas kernels: 105 us -> 103 us
    pallas_call x1, Pallas kernels: 105 us -> 103 us  [local(): pl.pallas_call(functools.partial(kernel, sizes), out_shape=pltpu.VMEM((fl...]
where the time goes in v4:
time: 105 us
  Pallas kernels  103 us (98%)
  local copies, waits for them, and re-layouts  2.02 us (2%)
    pallas_call x1, Pallas kernels, local(): pl.pallas_call(functools.partial(kernel, sizes), out_shape=pltpu.VMEM((fl...  103 us

profile of v4, /device:TPU:1, one launch (start us, length us, event | category | flops | bytes accessed | tf_op | source)
XLA Modules:
  0.0 104.6 jit_solution(16786802516478915712)
XLA Ops:
  0.0 102.6 %shard_map.73 = bf16[2,16,512,128]{3,2,1,0:T(8,128)(2,1)S(1)} custom-call(bf16[2,8,512,256]{3,2,1,0:T(8,128)(2,1)} %clip.1, bf16[256,256]{1,0:T(8,128)(2,1)} %wq_in.1, bf16[256,256]{1,0:T(8,128)(2,1)} %wk_in.1, bf16[256,256]{1,0:T(8,128)(2,1)} %wv_in.1, bf16[256,256]{1,0:T(8,128)(2,1)} %wo_in.1, bf16[3,768,256]{2,1,0:T(8,128)(2,1)} %bitcast.2, f32[1,256]{1,0:T(1,128)} %bitcast.3), custom_call_target="tpu_custom_call" | custom-call | flops 13958643712 | bytes 16777216 | tf_op jit(solution)/shard_map/pallas_call | solution.py:441
  102.6 2.0 %copy.9 = bf16[2,16,512,128]{3,2,1,0:T(8,128)(2,1)} copy(bf16[2,16,512,128]{3,2,1,0:T(8,128)(2,1)S(1)} %shard_map.73) | data formatting | bytes 8388608

commit v5 on v4

--- a/solution.py
+++ b/solution.py
@@ -213,6 +213,8 @@
     def _():
         pl.semaphore_signal(barrier, inc=1, device_id={"rows": strip + 1}, device_id_type=MESH)
 
+    whole = pltpu.make_async_copy(clip, clipv, clip_sem)
+    whole.start()
     for copy in weights:
         copy.start()
 
@@ -228,8 +230,6 @@
     def _(i):
         start_to_all(forward, order(i))
 
-    whole = pltpu.make_async_copy(clip, clipv, clip_sem)
-    whole.start()
     for copy in weights:
         copy.wait()
     wqv_t[:chans] = wq[...].astype(jnp.float32).T.astype(jnp.bfloat16)
@@ -359,8 +359,6 @@
         def _():
             halo(True).start()
 
-    whole.wait()
-
     @pl.loop(0, rows - 1 + LAG)
     def _(i):
         @pl.when(i < rows)
@@ -368,6 +366,10 @@
             attend(order(i))
 
         j = i - LAG
+
+        @pl.when(j == 0)
+        def _():
+            whole.wait()
 
         @pl.when(j >= 0)
         def _():

time: 105 us -> 105 us (level)
  no operation moved by 1% of the time
where the time goes in v5:
time: 105 us
  Pallas kernels  103 us (98%)
  local copies, waits for them, and re-layouts  2.02 us (2%)
    pallas_call x1, Pallas kernels, local(): pl.pallas_call(functools.partial(kernel, sizes), out_shape=pltpu.VMEM((fl...  103 us

profile of v5, /device:TPU:1, one launch (start us, length us, event | category | flops | bytes accessed | tf_op | source)
XLA Modules:
  0.0 104.6 jit_solution(8053342350202115331)
XLA Ops:
  0.0 102.6 %shard_map.73 = bf16[2,16,512,128]{3,2,1,0:T(8,128)(2,1)S(1)} custom-call(bf16[2,8,512,256]{3,2,1,0:T(8,128)(2,1)} %clip.1, bf16[256,256]{1,0:T(8,128)(2,1)} %wq_in.1, bf16[256,256]{1,0:T(8,128)(2,1)} %wk_in.1, bf16[256,256]{1,0:T(8,128)(2,1)} %wv_in.1, bf16[256,256]{1,0:T(8,128)(2,1)} %wo_in.1, bf16[3,768,256]{2,1,0:T(8,128)(2,1)} %bitcast.2, f32[1,256]{1,0:T(1,128)} %bitcast.3), custom_call_target="tpu_custom_call" | custom-call | flops 13958643712 | bytes 16777216 | tf_op jit(solution)/shard_map/pallas_call | solution.py:443
  102.6 2.0 %copy.9 = bf16[2,16,512,128]{3,2,1,0:T(8,128)(2,1)} copy(bf16[2,16,512,128]{3,2,1,0:T(8,128)(2,1)S(1)} %shard_map.73) | data formatting | bytes 8388608
